TPU v7x, 32 devices: a whole 2x2x4 slice. The times are simulated.
32 devices in a mesh: section: 4 (over z), expert: 8 (over y, x, core).
Axes of the slice: x: 2, y: 2, z: 4, core: 2. Of those that a mesh axis runs over, the one named last changes fastest.
Arguments:
- d_output: bfloat16 [4096, 4096], P(('section', 'expert')), may hold values from -3 to 3
- gate_values: bfloat16 [4096, 8], P(('section', 'expert')), may hold values from 0.049804688 to 0.5
- routes: int32 [4096, 8], P(('section', 'expert')), may hold values from 0 to 15, all different within a row; in each aligned block of 128 rows (0 to 127, 128 to 255, ...) at most 72 rows name the same one
- hidden_saved: bfloat16 [4, 16, 8, 72, 768], P('section', 'expert'), may hold values from -3 to 3
- w_down: bfloat16 [16, 768, 4096], P('expert'), may hold values from -0.21875 to 0.21875
Outputs:
- d_hidden: bfloat16 [4, 16, 8, 72, 768], P('section', 'expert')
- d_weight: bfloat16 [16, 768, 4096], P('expert', 'section')
- d_gate: float32 [4096, 8], P(('section', 'expert'))
Inputs may be any that keep to these rules, and one draw needn't show every extreme that they name: `routes`: each row names 8 different experts. Within the rows of one device (128 tokens) no expert is named by more than 72 rows, a bound that some block reaches.
All inputs are finite; a program needn't handle non-finite values.
Results may differ from a plain program's by a relative error of at most 0.017.
Values may be sent and summed in bfloat16 or wider, within the bound.
A program may use at most 192 MiB of HBM per device.

v0:
```python
import jax
import jax.numpy as jnp
from jax import lax
from jax.sharding import PartitionSpec as P


def slot_ranks(route_block, expert_count):
    one_hot = (route_block[..., None] == jnp.arange(expert_count, dtype=jnp.int32)).astype(
        jnp.int32
    )
    earlier = jnp.cumsum(one_hot, axis=1) - one_hot
    return jnp.sum(earlier * one_hot, axis=2)


def shards(d_output, gate_values, routes, hidden_saved, w_down):
    experts_held = w_down.shape[0]
    hidden_width = w_down.shape[1]
    model_width = d_output.shape[1]
    tok_rows = d_output.shape[0]
    top_count = gate_values.shape[1]
    capacity = hidden_saved.shape[3]
    expert_groups = lax.axis_size("expert")
    expert_count = experts_held * expert_groups
    slot_total = expert_count * capacity
    route_list = routes.reshape(-1)
    slot_rank = slot_ranks(route_list[None, :], expert_count)[0]
    slot_index = (
        route_list % experts_held * (expert_groups * capacity)
        + route_list // experts_held * capacity
        + slot_rank
    )
    pair_total = tok_rows * top_count
    source_pair = (
        jnp.full((slot_total + 1,), pair_total, jnp.int32)
        .at[slot_index]
        .set(jnp.arange(pair_total, dtype=jnp.int32))[:slot_total]
    )
    dy_padded = jnp.concatenate([d_output, jnp.zeros((1, model_width), jnp.bfloat16)], axis=0)
    gate_padded = jnp.concatenate([gate_values.reshape(-1), jnp.zeros((1,), jnp.bfloat16)], axis=0)
    dy_slots = dy_padded[source_pair // top_count].reshape(
        experts_held, expert_groups, capacity, model_width
    )
    gate_slots = gate_padded[source_pair].reshape(experts_held, expert_groups, capacity)
    got_dy, got_gate = (
        lax.all_to_all(dy_slots, "expert", split_axis=1, concat_axis=1, tiled=True),
        lax.all_to_all(gate_slots, "expert", split_axis=1, concat_axis=1, tiled=True),
    )
    gated_rows = (got_gate.astype(jnp.float32)[..., None] * got_dy.astype(jnp.float32)).astype(
        jnp.bfloat16
    )
    gated_rows = gated_rows.reshape(experts_held, expert_groups * capacity, model_width)
    hidden = hidden_saved.reshape(experts_held, expert_groups * capacity, hidden_width)
    d_hidden = jnp.einsum(
        "lrd,lfd->lrf", gated_rows, w_down, preferred_element_type=jnp.float32
    ).astype(jnp.bfloat16)
    partial_value = jnp.einsum(
        "lrf,lrd->lfd", hidden, gated_rows, preferred_element_type=jnp.float32
    )
    d_weight = lax.psum_scatter(
        partial_value.astype(jnp.bfloat16), "section", scatter_dimension=1, tiled=True
    )
    expert_rows = jnp.einsum(
        "lrf,lfd->lrd", hidden, w_down, preferred_element_type=jnp.float32
    ).astype(jnp.bfloat16)
    returned = lax.all_to_all(
        expert_rows.reshape(experts_held, expert_groups, capacity, model_width),
        "expert",
        split_axis=1,
        concat_axis=1,
        tiled=True,
    )
    picked = returned.reshape(-1, model_width)[slot_index].reshape(tok_rows, top_count, model_width)
    d_gate = jnp.sum(d_output.astype(jnp.float32)[:, None, :] * picked.astype(jnp.float32), axis=2)
    return (d_hidden.reshape(hidden_saved.shape), d_weight, d_gate)


def solution(mesh):
    placed = (
        P(("section", "expert"), None),
        P(("section", "expert"), None),
        P(("section", "expert"), None),
        P("section", "expert", None, None, None),
        P("expert", None, None),
    )
    return jax.shard_map(
        shards,
        mesh=mesh,
        in_specs=placed,
        out_specs=(
            P("section", "expert", None, None, None),
            P("expert", "section", None),
            P(("section", "expert"), None),
        ),
        check_vma=False,
    )
```

profile of v0, /device:TPU:0, one launch (start us, length us, event | category | flops | bytes accessed | tf_op | source)
XLA Modules:
  0.0 663.5 jit_solution(11730212551435935900)
XLA Ops:
  8.2 4.5 reduce-window.6
  13.4 4.3 scatter_custom_fusion
  18.7 7.3 %gather_fusion = bf16[1152]{0:T(1024)(128)(2,1)S(1)} fusion(bf16[1025]{0:T(1024)(128)(2,1)S(1)} %pad_maximum_fusion, s32[2048]{0:T(1024)S(1)} %get-tuple-element.23), kind=kCustom, calls=%fused_computation | custom fusion | bytes 9216 | tf_op jit(solution)/shard_map/gather | solution.py:43
  26.7 5.2 all-to-all-start
  31.8 1.3 concatenate.7
  33.2 8.0 %gather_fusion.1 = bf16[1152,4096]{1,0:T(8,128)(2,1)} fusion(bf16[129,4096]{1,0:T(8,128)(2,1)S(1)} %concatenate.7, s32[2048]{0:T(1024)S(1)} %get-tuple-element.22), kind=kCustom, calls=%fused_computation.1 | custom fusion | bytes 18878976 | tf_op jit(solution)/shard_map/gather | solution.py:40
  41.2 8.7 %copy.49 = bf16[2,8,72,4096]{3,2,0,1:T(8,128)(2,1)} copy(bf16[2,8,72,4096]{3,2,1,0:T(8,128)(2,1)} %bitcast.37) | data formatting | bytes 18874368 | tf_op jit(solution)/shard_map/reshape | solution.py:40
  49.9 5.0 all-to-all-start.1
  55.2 105.2 %all-to-all-done.1 = bf16[2,8,72,4096]{3,2,0,1:T(8,128)(2,1)} async-done(((bf16[2,8,72,4096]{3,2,0,1:T(8,128)(2,1)}), bf16[2,8,72,4096]{3,2,0,1:T(8,128)(2,1)}, u32[]{:S(2)}, u32[]{:S(2)}) %all-to-all-start.1) | async-done | bytes 9437216 | tf_op jit(solution)/shard_map/all_to_all | solution.py:45
  160.4 11.2 %multiply_convert_fusion = bf16[2,8,72,4096]{3,2,1,0:T(8,128)(2,1)} fusion(bf16[2,8,72,4096]{3,2,0,1:T(8,128)(2,1)} %all-to-all-done.1, f32[2,8,72]{2,1,0:T(8,128)S(1)} %copy_convert_fusion), kind=kLoop, calls=%fused_computation.4 | loop fusion | flops 14155776 | bytes 18878976 | tf_op jit(solution)/shard_map/convert_element_type | solution.py:48
  171.6 19.2 %convert_bitcast_fusion = bf16[2,768,4096]{1,2,0:T(8,128)(2,1)} fusion(bf16[2,576,4096]{2,1,0:T(8,128)(2,1)} %bitcast.38, bf16[2,576,768]{2,1,0:T(8,128)(2,1)S(1)} %bitcast.34), kind=kOutput, calls=%fused_computation.7 | convolution fusion | flops 7254048768 | bytes 23789568 | tf_op jit(solution)/shard_map/lrf,lrd->lfd/dot_general | solution.py:56
  190.8 31.6 %copy.51 = bf16[2,768,4096]{2,0,1:T(2,128)(2,1)} copy(bf16[2,768,4096]{1,2,0:T(8,128)(2,1)} %convert_bitcast_fusion) | data formatting | bytes 25165824 | tf_op jit(solution)/shard_map/convert_element_type | solution.py:60
  222.3 14.2 %convolution_convert_fusion = bf16[2,576,4096]{2,1,0:T(8,128)(2,1)} fusion(bf16[2,576,768]{2,1,0:T(8,128)(2,1)S(1)} %bitcast.35, bf16[2,768,4096]{2,1,0:T(8,128)(2,1)} %param.9), kind=kOutput, calls=%fused_computation.8 | convolution fusion | flops 7252475904 | bytes 23789568 | tf_op jit(solution)/shard_map/lrf,lfd->lrd/dot_general | solution.py:62
  236.6 8.7 %copy.52 = bf16[2,8,72,4096]{3,2,0,1:T(8,128)(2,1)} copy(bf16[2,8,72,4096]{3,2,1,0:T(8,128)(2,1)} %bitcast.40) | data formatting | bytes 18874368 | tf_op jit(solution)/shard_map/reshape | solution.py:66
  245.3 5.4 all-to-all-start.2
  250.8 1.5 convert_element_type.52
  253.5 102.3 %all-to-all-done.2 = bf16[2,8,72,4096]{3,2,0,1:T(8,128)(2,1)} async-done(((bf16[2,8,72,4096]{3,2,0,1:T(8,128)(2,1)}), bf16[2,8,72,4096]{3,2,0,1:T(8,128)(2,1)}, u32[]{:S(2)}, u32[]{:S(2)}) %all-to-all-start.2) | async-done | bytes 9437216 | tf_op jit(solution)/shard_map/all_to_all | solution.py:65
  355.8 8.8 %copy.53 = bf16[2,8,72,4096]{3,2,1,0:T(8,128)(2,1)} copy(bf16[2,8,72,4096]{3,2,0,1:T(8,128)(2,1)} %all-to-all-done.2) | data formatting | bytes 18874368 | tf_op jit(solution)/shard_map/all_to_all | solution.py:65
  364.6 20.0 %gather_fusion.2 = bf16[1024,4096]{1,0:T(8,128)(2,1)} fusion(bf16[1152,4096]{1,0:T(8,128)(2,1)} %bitcast.36, s32[1024]{0:T(1024)S(1)} %broadcast_clamp_fusion), kind=kCustom, calls=%fused_computation.2 | custom fusion | bytes 16781312 | tf_op jit(solution)/shard_map/gather | solution.py:72
  384.6 5.7 fusion
  390.9 14.7 %convolution_convert_fusion.1 = bf16[2,576,768]{2,1,0:T(8,128)(2,1)} fusion(bf16[2,576,4096]{2,1,0:T(8,128)(2,1)} %bitcast.39, bf16[2,768,4096]{2,1,0:T(8,128)(2,1)} %param.9), kind=kOutput, calls=%fused_computation.9 | convolution fusion | flops 7248642048 | bytes 23789568 | tf_op jit(solution)/shard_map/lrd,lfd->lrf/dot_general | solution.py:53
  405.7 242.3 %all-reduce.4.cloned.1.call-done = bf16[2,768,4096]{2,0,1:T(2,128)(2,1)} async-done(((bf16[2,768,4096]{2,0,1:T(2,128)(2,1)}), bf16[2,768,4096]{2,0,1:T(2,128)(2,1)}) %all-reduce.4.cloned.1.call-update) | async-done | bytes 12582928
  648.0 4.9 constant_dynamic-slice_fusion
  652.9 3.8 copy.54
  (39 shorter events, 4.8 us)
Async XLA Ops:
  7.2 164.4 %copy-start = (bf16[1,2,8,72,768]{4,3,2,1,0:T(8,128)(2,1)S(1)}, bf16[1,2,8,72,768]{4,3,2,1,0:T(8,128)(2,1)}, u32[]{:S(2)}) copy-start(bf16[1,2,8,72,768]{4,3,2,1,0:T(8,128)(2,1)} %param.8) | copy-start | bytes 5308420
  26.7 23.3 %all-to-all-start = ((bf16[2,8,72]{2,0,1:T(2,128)(2,1)}), bf16[2,8,72]{2,0,1:T(2,128)(2,1)S(1)}, u32[]{:S(2)}, u32[]{:S(2)}) async-start(bf16[2,8,72]{2,0,1:T(2,128)(2,1)} %copy.47), calls=%async_computation | async-start | bytes 8192 | tf_op jit(solution)/shard_map/all_to_all | solution.py:46
  49.9 110.4 %all-to-all-start.1 = ((bf16[2,8,72,4096]{3,2,0,1:T(8,128)(2,1)}), bf16[2,8,72,4096]{3,2,0,1:T(8,128)(2,1)}, u32[]{:S(2)}, u32[]{:S(2)}) async-start(bf16[2,8,72,4096]{3,2,0,1:T(8,128)(2,1)} %copy.49), calls=%async_computation.1 | async-start | bytes 18874368 | tf_op jit(solution)/shard_map/all_to_all | solution.py:45
  55.0 593.0 %all-reduce.4.cloned.1.call-start = ((), (), s32[]{:S(2)}) async-start(), calls=%async_computation.3 | async-start | bytes 25165824
  245.3 5.5 copy-start.2
  245.3 7.0 %copy-start.3 = (u32[32]{0:T(128)S(1)}, u32[32]{0:T(128)}, u32[]{:S(2)}) copy-start(u32[32]{0:T(128)} %constant.72) | copy-start | bytes 388
  245.3 110.5 %all-to-all-start.2 = ((bf16[2,8,72,4096]{3,2,0,1:T(8,128)(2,1)}), bf16[2,8,72,4096]{3,2,0,1:T(8,128)(2,1)}, u32[]{:S(2)}, u32[]{:S(2)}) async-start(bf16[2,8,72,4096]{3,2,0,1:T(8,128)(2,1)} %copy.52), calls=%async_computation.2 | async-start | bytes 18874368 | tf_op jit(solution)/shard_map/all_to_all | solution.py:65
  390.9 265.8 %copy-start.1 = (bf16[1,2,8,72,768]{4,3,2,1,0:T(8,128)(2,1)S(1)}, bf16[1,2,8,72,768]{4,3,2,1,0:T(8,128)(2,1)}, u32[]{:S(2)}) copy-start(bf16[1,2,8,72,768]{4,3,2,1,0:T(8,128)(2,1)} %param.8) | copy-start | bytes 5308420
Sparse Core Ops, SparseCore 0:
  222.5 425.4 all-reduce.3
where the time goes:
time: 665 us; the launch traced here: 664 us
  waiting for transfers between devices  450 us (68%)
  local copies, waits for them, and re-layouts  112 us (17%)
  matrix products  48.2 us (7%)
  other arithmetic  23.1 us (3%)
  starting transfers between devices  15.9 us (2%)
  between operations  14.9 us (2%)
    unnamed x2, waiting for transfers between devices  242 us
    all_to_all x1, waiting for transfers between devices, shards(): lax.all_to_all(dy_slots, 'expert', split_axis=1, concat_axis=1, tiled=True)  105 us
    all_to_all x1, waiting for transfers between devices, shards(): lax.all_to_all(expert_rows.reshape(experts_held, expert_groups, capacity,...  102 us
    convert_element_type x1, local copies, waits for them, and re-layouts, shards(): partial_value.astype(jnp.bfloat16)  31.6 us
    gather x1, local copies, waits for them, and re-layouts, shards(): returned.reshape(-1, model_width)[slot_index]  20 us
    dot_general x1, matrix products, shards(): jnp.einsum('lrf,lrd->lfd', hidden, gated_rows, preferred_element_type=jnp...  19.2 us
    dot_general x1, matrix products, shards(): jnp.einsum('lrd,lfd->lrf', gated_rows, w_down, preferred_element_type=jnp...  14.7 us
    dot_general x1, matrix products, shards(): jnp.einsum('lrf,lfd->lrd', hidden, w_down, preferred_element_type=jnp.flo...  14.2 us
  transfers between devices with their start and end apart: 4, of which 3 were waited for; matrix products, arithmetic and copies ran while one was open for 14% of the time, Pallas kernels for 0%

commit v1 on v0

v1 whole, which is shorter than its diff:
```python
import jax
import jax.numpy as jnp
from jax import lax
from jax.sharding import PartitionSpec as P


def shards(d_output, gate_values, routes, hidden_saved, w_down):
    held, hidden_width, width = w_down.shape
    tok = d_output.shape[0]
    sources, capacity = hidden_saved.shape[2], hidden_saved.shape[3]
    sections = lax.axis_size("section")
    expert_count = held * sources
    me = lax.axis_index("expert")
    f32, bf16 = jnp.float32, jnp.bfloat16

    match = routes[:, :, None] == jnp.arange(expert_count, dtype=jnp.int32)
    chosen = jnp.any(match, axis=1).astype(jnp.int32)
    rank = jnp.where(chosen > 0, jnp.cumsum(chosen, axis=0) - chosen, -1)
    gate = jnp.sum(jnp.where(match, gate_values[:, :, None].astype(f32), 0.0), axis=1)
    table = jnp.stack([rank.T.astype(bf16), gate.T.astype(bf16)])
    table = lax.all_gather(table, ("section", "expert"))
    mine = lax.dynamic_slice_in_dim(table, me * held, held, axis=2)
    mine = mine.reshape(sections, sources, 2, held, tok)

    by_section = lax.all_gather(d_output, "section")
    dy = lax.all_gather(by_section, "expert", axis=1)

    blocks = hidden_saved[0].reshape(held, sources, capacity, sections, -1)
    blocks = jnp.transpose(blocks, (3, 0, 1, 2, 4))
    parts = lax.all_to_all(blocks, "section", split_axis=0, concat_axis=0, tiled=True)

    slots = jnp.arange(capacity, dtype=jnp.int32)
    slot_of = mine[:, :, 0].astype(jnp.int32)
    pick = (slot_of[..., None] == slots) * mine[:, :, 1].astype(f32)[..., None]
    scattered = jnp.einsum(
        "sjetc,sejcf->sjtef", pick.astype(bf16), parts, preferred_element_type=f32
    ).astype(bf16)
    d_weight = jnp.einsum("sjtef,sjtd->efd", scattered, dy, preferred_element_type=f32).astype(
        bf16
    )

    own = lax.axis_index("section")
    dy_own = lax.dynamic_index_in_dim(dy, own, 0, keepdims=False)
    rank_own = lax.dynamic_index_in_dim(slot_of, own, 0, keepdims=False)
    gate_own = lax.dynamic_index_in_dim(mine[:, :, 1], own, 0, keepdims=False)
    select = rank_own[:, :, None, :] == slots[:, None]
    gate_slot = jnp.sum(jnp.where(select, gate_own.astype(f32)[:, :, None, :], 0.0), axis=3)
    rows = jnp.einsum(
        "ject,jtd->ejcd", select.astype(bf16), dy_own, preferred_element_type=f32
    ).astype(bf16)
    plain = jnp.einsum("ejcd,efd->ejcf", rows, w_down, preferred_element_type=f32)
    gate_ejc = jnp.transpose(gate_slot, (1, 0, 2))
    d_hidden = (plain * gate_ejc[..., None]).astype(bf16)[None]
    value = jnp.sum(plain * hidden_saved[0].astype(f32), axis=3)
    token_value = jnp.sum(
        jnp.where(select, jnp.transpose(value, (1, 0, 2))[..., None], 0.0), axis=2
    )
    back = lax.all_to_all(token_value, "expert", split_axis=0, concat_axis=0, tiled=True)
    back = back.reshape(expert_count, tok)
    d_gate = jnp.sum(jnp.where(match, back.T[:, None, :], 0.0), axis=2)
    return d_hidden, d_weight, d_gate


def solution(mesh):
    placed = (
        P(("section", "expert"), None),
        P(("section", "expert"), None),
        P(("section", "expert"), None),
        P("section", "expert", None, None, None),
        P("expert", None, None),
    )
    return jax.shard_map(
        shards,
        mesh=mesh,
        in_specs=placed,
        out_specs=(
            P("section", "expert", None, None, None),
            P("expert", "section", None),
            P(("section", "expert"), None),
        ),
        check_vma=False,
    )
```

time: 665 us -> 306 us (0.46)
  waiting for transfers between devices: 450 us -> 156 us
  local copies, waits for them, and re-layouts: 112 us -> 7.35 us
  blocking collectives: 0 us -> 78.3 us
  other arithmetic: 23.1 us -> 4.89 us
  matrix products: 48.2 us -> 36.9 us
  starting transfers between devices: 15.9 us -> 7.91 us
    unnamed x2, waiting for transfers between devices: 242 us -> 0.7 us
    all_to_all x3 -> x2, waiting for transfers between devices: 207 us -> 0.01 us  [the longest x1 0.01 us: shards(): lax.all_to_all(token_value, 'expert', split_axis=0, concat_axis=0, tiled=...]
    all_gather x0 -> x2, waiting for transfers between devices: none -> 155 us  [the longest x1 85.1 us: shards(): by_section = lax.all_gather(d_output, 'section')]
    all_gather x0 -> x1, blocking collectives: none -> 78.3 us  [shards(): table = lax.all_gather(table, ('section', 'expert'))]
    gather x3 -> x0, local copies, waits for them, and re-layouts: 35.3 us -> none  [the longest x1 20 us: shards(): returned.reshape(-1, model_width)[slot_index]]
    convert_element_type x1 -> x2, local copies, waits for them, and re-layouts: 31.6 us -> 0.02 us  [the longest x1 0.01 us: shards(): slot_of = mine[:, :, 0].astype(jnp.int32)]
    reshape x6 -> x0, local copies, waits for them, and re-layouts: 18.3 us -> none  [the longest x1 8.72 us: shards(): expert_rows.reshape(experts_held, expert_groups, capacity, model_width)]
    convert_element_type x3 -> x4, other arithmetic: 12.7 us -> 0.63 us  [the longest x1 0.6 us: shards(): gate_own.astype(f32)[:, :, None, :]]
  transfers between devices with their start and end apart: 4 -> 4, of which waited for: 3 -> 2; matrix products, arithmetic and copies ran while one was open for 14% -> 10% of each run, Pallas kernels for 0% -> 0%
where the time goes in v1:
time: 306 us; the launch traced here: 305 us
  waiting for transfers between devices  156 us (51%)
  blocking collectives  78.3 us (26%)
  matrix products  36.9 us (12%)
  between operations  14.2 us (5%)
  starting transfers between devices  7.91 us (3%)
  local copies, waits for them, and re-layouts  7.35 us (2%)
  other arithmetic  4.89 us (2%)
    all_gather x1, waiting for transfers between devices, shards(): by_section = lax.all_gather(d_output, 'section')  85.1 us
    all_gather x1, blocking collectives, shards(): table = lax.all_gather(table, ('section', 'expert'))  78.3 us
    all_gather x1, waiting for transfers between devices, shards(): dy = lax.all_gather(by_section, 'expert', axis=1)  70 us
    dot_general x1, matrix products, shards(): jnp.einsum('sjtef,sjtd->efd', scattered, dy, preferred_element_type=f32)  19.2 us
    dot_general x1, matrix products, shards(): jnp.einsum('ejcd,efd->ejcf', rows, w_down, preferred_element_type=f32)  15 us
  transfers between devices with their start and end apart: 4, of which 2 were waited for; matrix products, arithmetic and copies ran while one was open for 10% of the time, Pallas kernels for 0%

profile of v1, /device:TPU:0, one launch (start us, length us, event | category | flops | bytes accessed | tf_op | source)
XLA Modules:
  0.0 305.3 jit_solution(6787586456683879704)
XLA Ops:
  7.2 0.0 all-gather.6.cloned.1.call-start
  7.2 0.7 all-gather.6.cloned.1.call-update
  7.9 0.0 all-gather.8.cloned.1.call-start
  7.9 85.1 %all-gather.6.cloned.1.call-done = bf16[512,4096]{1,0:T(8,128)(2,1)} async-done(((bf16[128,4096]{1,0:T(8,128)(2,1)}), bf16[512,4096]{1,0:T(8,128)(2,1)}) %all-gather.6.cloned.1.call-update) | async-done | bytes 4194320 | tf_op jit(solution)/shard_map/all_gather | solution.py:25
  93.1 0.0 all-gather.8.cloned.1.call-update
  93.1 4.8 %reshape_squeeze.3 = bf16[2,8,72,4,192]{4,3,2,1,0:T(4,128)(2,1)S(1)} reshape(bf16[1,2,8,72,768]{4,3,2,1,0:T(8,128)(2,1)} %param.8) | data formatting | bytes 3538944 | tf_op jit(solution)/shard_map/reshape;squeeze | solution.py:28
  97.9 1.7 copy.87
  99.6 3.9 %all-to-all-start = ((bf16[4,2,8,72,192]{4,3,2,1,0:T(8,128)(2,1)}), bf16[4,2,8,72,192]{4,3,2,1,0:T(8,128)(2,1)S(1)}, u32[]{:S(2)}, u32[]{:S(2)}) async-start(bf16[4,2,8,72,192]{4,3,2,1,0:T(8,128)(2,1)} %copy.87), calls=%async_computation | async-start | bytes 4718592 | tf_op jit(solution)/shard_map/all_to_all | solution.py:30
  103.6 0.1 copy.80
  103.7 0.2 reduce_window_sum.11
  103.9 0.1 copy.81
  104.0 78.3 %all-gather.2 = bf16[64,16,128]{2,1,0:T(8,128)(2,1)S(1)} all-gather(bf16[2,16,128]{2,1,0:T(8,128)(2,1)S(1)} %pad_maximum_fusion), channel_id=4, replica_groups=mesh['section'=4,'expert'=8] {'section','expert'}, dimensions={0}, use_global_device_ids=true | all-gather | bytes 270336 | tf_op jit(solution)/shard_map/all_gather | solution.py:21
  182.4 0.6 bitcast_convert_fusion.2
  183.0 0.0 all-to-all-done
  183.0 2.7 fusion.46
  185.7 70.0 %all-gather.8.cloned.1.call-done = bf16[4,1024,4096]{2,1,0:T(8,128)(2,1)} async-done(((bf16[4,128,4096]{2,1,0:T(8,128)(2,1)}), bf16[4,1024,4096]{2,1,0:T(8,128)(2,1)}) %all-gather.8.cloned.1.call-update) | async-done | bytes 33554448 | tf_op jit(solution)/shard_map/all_gather | solution.py:26
  255.8 15.0 %fusion.15 = (f32[2,8,72]{2,1,0:T(8,128)}, f32[2,8,72,768]{3,2,1,0:T(8,128)S(1)}) fusion(bf16[1,2,8,72,768]{4,3,2,1,0:T(8,128)(2,1)} %param.8, bf16[2,768,4096]{2,1,0:T(8,128)(2,1)} %param.9, bf16[4,8,128,4096]{3,2,1,0:T(8,128)(2,1)} %bitcast.86, s32[]{:T(128)S(6)} %select_n.33, s32[8,2,128]{2,0,1:T(8,128)S(1)} %dynamic-slice_bitcast_fusion), kind=kOutput, calls=%fused_computation.12 | convolution fusion | flops 8463236096 | bytes 26292740 | tf_op jit(solution)/shard_map/ejcd,efd->ejcf/dot_general | solution.py:51
  270.8 1.3 select_reduce_fusion
  272.0 0.6 copy.91
  272.6 3.9 %all-to-all-start.1 = ((f32[8,2,128]{2,1,0:T(2,128)}), f32[8,2,128]{2,1,0:T(2,128)}, u32[]{:S(2)}, u32[]{:S(2)}) async-start(f32[8,2,128]{2,1,0:T(2,128)} %copy.91), calls=%async_computation.1 | async-start | bytes 16384 | tf_op jit(solution)/shard_map/all_to_all | solution.py:58
  276.6 19.2 %bitcast_convert_fusion = bf16[2,192,4096]{2,1,0:T(8,128)(2,1)} fusion(bf16[4,8,128,4096,1]{3,2,1,0,4:T(8,128)(2,1)} %bitcast.87, bf16[4,8,128,2,192]{2,4,0,1,3:T(8,128)(2,1)} %fusion.46), kind=kOutput, calls=%fused_computation.10 | convolution fusion | flops 12886474752 | bytes 39845888 | tf_op jit(solution)/shard_map/sjtef,sjtd->efd/dot_general | solution.py:38
  295.7 1.5 fusion.22
  297.2 0.0 all-to-all-done.1
  297.2 1.3 select_reduce_fusion.2
  (18 shorter events, 0.2 us)
Async XLA Ops:
  7.2 85.9 %all-gather.6.cloned.1.call-start = ((), (), s32[]{:S(2)}) async-start(), calls=%async_computation.2 | async-start | bytes 5242880 | tf_op jit(solution)/shard_map/all_gather | solution.py:25
  7.9 247.9 %all-gather.8.cloned.1.call-start = ((), (), s32[]{:S(2)}) async-start(), calls=%async_computation.3 | async-start | bytes 37748736 | tf_op jit(solution)/shard_map/all_gather | solution.py:26
  99.6 3.9 %copy-start.2 = (bf16[128,8]{0,1:T(8,128)(2,1)S(1)}, bf16[128,8]{0,1:T(8,128)(2,1)}, u32[]{:S(2)}) copy-start(bf16[128,8]{0,1:T(8,128)(2,1)} %param.6) | copy-start | bytes 6148
  99.6 4.0 %copy-start = (s32[128,8]{0,1:T(8,128)S(1)}, s32[128,8]{0,1:T(8,128)}, u32[]{:S(2)}) copy-start(s32[128,8]{0,1:T(8,128)} %param.7) | copy-start | bytes 12292
  99.6 83.5 %all-to-all-start = ((bf16[4,2,8,72,192]{4,3,2,1,0:T(8,128)(2,1)}), bf16[4,2,8,72,192]{4,3,2,1,0:T(8,128)(2,1)S(1)}, u32[]{:S(2)}, u32[]{:S(2)}) async-start(bf16[4,2,8,72,192]{4,3,2,1,0:T(8,128)(2,1)} %copy.87), calls=%async_computation | async-start | bytes 4718592 | tf_op jit(solution)/shard_map/all_to_all | solution.py:30
  182.4 88.4 %copy-start.1 = (s32[8,2,128]{2,0,1:T(8,128)}, s32[8,2,128]{2,0,1:T(8,128)S(1)}, u32[]{:S(2)}) copy-start(s32[8,2,128]{2,0,1:T(8,128)S(1)} %dynamic-slice_bitcast_fusion) | copy-start | bytes 24580
  272.6 24.6 %all-to-all-start.1 = ((f32[8,2,128]{2,1,0:T(2,128)}), f32[8,2,128]{2,1,0:T(2,128)}, u32[]{:S(2)}, u32[]{:S(2)}) async-start(f32[8,2,128]{2,1,0:T(2,128)} %copy.91), calls=%async_computation.1 | async-start | bytes 16384 | tf_op jit(solution)/shard_map/all_to_all | solution.py:58
Sparse Core Ops, SparseCore 0:
  9.6 83.4 all-gather.5
  95.0 160.7 all-gather.7

commit v2 on v1

v2 whole, which is shorter than its diff:
```python
import functools

import jax
import jax.numpy as jnp
from jax import lax
from jax.experimental import pallas as pl
from jax.experimental.pallas import tpu as pltpu
from jax.sharding import PartitionSpec as P

MESH = pl.DeviceIdType.MESH
TILE = 512


def flipped(index, bits):
    for bit in bits:
        index = index + bit * (1 - 2 * ((index // bit) % 2))
    return index


def dot(a, b, dims):
    return lax.dot_general(a, b, (dims, ((), ())), preferred_element_type=jnp.float32)


def body(sections, sources, dy_ref, tab_ref, hid_ref, blocks_ref, w_ref,
         all_ref, dw_ref, dh_ref, back_ref,
         tabs, parts, dy_vm, w_vm, acc, scattered, picked, rows_vm, plain, token_vm, back_vm,
         local_sem, z_send, z_recv, h_send, h_recv, e_send, e_recv, b_send, b_recv):
    f32, bf16 = jnp.float32, jnp.bfloat16
    z, j = lax.axis_index("section"), lax.axis_index("expert")
    tok, width = dy_ref.shape
    held, slot_rows, hidden_width = hid_ref.shape
    pairs = sources // 2
    pair_rows = slot_rows // pairs
    capacity = pair_rows // 2
    part_width = blocks_ref.shape[2] // held
    expert_count = tab_ref.shape[0] // 2
    half_rows = tok // 2
    bits = [1 << b for b in range(sources.bit_length() - 1)]
    orders = (bits[1:] + bits[:1], bits[1:][::-1] + bits[:1])
    steps = [0]
    for d in range(1, sections):
        steps.append((d + 1) // 2 if d % 2 else sections - d // 2)

    def section_at(i):
        return (z + sections - steps[i]) % sections

    tabs[z, j] = tab_ref[...]
    barrier = pltpu.get_barrier_semaphore()
    for d in range(1, sections):
        pl.semaphore_signal(barrier, inc=1, device_id=((z + d) % sections, j), device_id_type=MESH)
    for r in range(1, sources):
        pl.semaphore_signal(barrier, inc=1, device_id=(z, (j + r) % sources), device_id_type=MESH)
    pl.semaphore_wait(barrier, sections + sources - 2)

    own_dy = pltpu.make_async_copy(dy_ref, all_ref.at[z, pl.ds(pl.multiple_of(j * tok, tok), tok)], local_sem.at[0])
    own_hid = pltpu.make_async_copy(blocks_ref.at[z], parts.at[z], local_sem.at[1])
    get_w = pltpu.make_async_copy(w_ref, w_vm, local_sem.at[2])

    def remote(source, target, send, recv, to):
        return pltpu.make_async_remote_copy(
            source, target, send, recv, device_id=to, device_id_type=MESH)

    def block_at(s, block, start, count):
        return all_ref.at[s, pl.ds(pl.multiple_of(block * tok + start, 16), count)]

    z_copies, h_copies = [None], [None]
    for i in range(1, sections):
        to = (z + steps[i]) % sections
        z_copies.append([
            remote(dy_ref, block_at(z, j, 0, tok), z_send.at[i, 0], z_recv.at[i, 0], (to, j)),
            remote(tabs.at[z, j], tabs.at[z, j], z_send.at[i, 1], z_recv.at[i, 1], (to, j)),
        ])
        h_copies.append(remote(blocks_ref.at[to], parts.at[z], h_send.at[i], h_recv.at[i], (to, j)))

    stage = {}

    def begin(i, k):
        s = section_at(i)
        stage[i, k] = []
        for part in range(3):
            order = orders[part % 2]
            have = [[]]
            for bit in order[:k]:
                have = have + [r + [bit] for r in have]
            to = (z, flipped(j, [order[k]]))
            for r in have:
                block = flipped(j, r)
                slot = sum(r) + order[k]
                sems = e_send.at[i, part, slot], e_recv.at[i, part, slot]
                if part == 2:
                    copy = remote(tabs.at[s, block], tabs.at[s, block], *sems, to)
                else:
                    target = block_at(s, block, part * half_rows, half_rows)
                    source = target
                    if i == 0 and not r:
                        source = dy_ref.at[pl.ds(part * half_rows, half_rows)]
                    copy = remote(source, target, *sems, to)
                copy.start()
                stage[i, k].append(copy)

    def arrive(i, k):
        for copy in stage[i, k]:
            copy.wait_recv()

    last = len(bits) - 1

    def fetch(i):
        load = pltpu.make_async_copy(all_ref.at[section_at(i)], dy_vm, local_sem.at[3])
        load.start()
        load.wait()

    def row_of(i, p, row):
        s = section_at(i)
        return jnp.concatenate(
            [tabs[s, 2 * p, pl.ds(row, 1), :], tabs[s, 2 * p + 1, pl.ds(row, 1), :]], axis=1)

    def rank_row(i, p, e):
        rank = row_of(i, p, j * held + e)
        lane = lax.broadcasted_iota(jnp.int32, rank.shape, 1)
        return jnp.where(rank < 0, -1.0, rank + jnp.where(lane < tok, 0.0, float(capacity)))

    def gate_row(i, p, e):
        return row_of(i, p, expert_count + j * held + e)

    def chosen(i, p, e):
        place = lax.broadcasted_iota(jnp.int32, (pair_rows, 2 * tok), 0).astype(f32)
        return place == rank_row(i, p, e)

    def weight_part(i):
        s = section_at(i)
        for p in range(pairs):
            hid = parts[s, p * pair_rows:(p + 1) * pair_rows, :]
            for e in range(held):
                gates = jnp.where(chosen(i, p, e), gate_row(i, p, e), 0.0).astype(bf16)
                moved = dot(hid, gates, ((0,), (0,)))
                scattered[e * part_width:(e + 1) * part_width, p * 2 * tok:(p + 1) * 2 * tok] = (
                    moved[e * part_width:(e + 1) * part_width].astype(bf16))

        def tile(t, _):
            cols = pl.ds(pl.multiple_of(t * TILE, TILE), TILE)
            value = dot(scattered[...], dy_vm[:, cols], ((1,), (0,)))
            if i > 0:
                value = value + acc[:, cols]
            if i == sections - 1:
                dw_ref[:, cols] = value.astype(bf16)
            else:
                acc[:, cols] = value
            return 0

        lax.fori_loop(0, width // TILE, tile, 0)

    def hidden_part():
        for e in range(held):
            for p in range(pairs):
                picked[e, p] = jnp.where(chosen(0, p, e), 1.0, 0.0).astype(bf16)
            plain[e] = jnp.zeros(plain.shape[1:], f32)

        def tile(t, _):
            cols = pl.ds(pl.multiple_of(t * TILE, TILE), TILE)
            for e in range(held):
                for p in range(pairs):
                    rows_vm[p * pair_rows:(p + 1) * pair_rows, :] = dot(
                        picked[e, p], dy_vm[p * 2 * tok:(p + 1) * 2 * tok, cols], ((1,), (0,))
                    ).astype(bf16)
                plain[e] += dot(rows_vm[...], w_vm[e, :, cols], ((1,), (1,)))
            return 0

        lax.fori_loop(0, width // TILE, tile, 0)
        for e in range(held):
            for p in range(pairs):
                rows = slice(p * pair_rows, (p + 1) * pair_rows)
                here = chosen(0, p, e)
                gate = jnp.sum(jnp.where(here, gate_row(0, p, e), 0.0), axis=1, keepdims=True)
                value = plain[e, rows, :]
                dh_ref[e, rows, :] = (value * gate).astype(bf16)
                total = jnp.sum(value * hid_ref[e, rows, :].astype(f32), axis=1, keepdims=True)
                by_token = jnp.sum(jnp.where(here, total, 0.0), axis=0, keepdims=True)
                token_vm[2 * p, e:e + 1, :] = by_token[:, :tok]
                token_vm[2 * p + 1, e:e + 1, :] = by_token[:, tok:]

    b_copies = []
    for r in range(1, sources):
        to = (j + r) % sources
        b_copies.append(remote(token_vm.at[to], back_vm.at[j], b_send.at[r], b_recv.at[r], (z, to)))

    token_vm[...] = jnp.zeros(token_vm.shape, f32)
    begin(0, 0)
    own_dy.start()
    own_hid.start()
    get_w.start()
    if sections > 1:
        for copy in z_copies[1]:
            copy.start()
        h_copies[1].start()
    for i in range(sections):
        for k in range(1, last):
            arrive(i, k - 1)
            begin(i, k)
        if i + 1 < sections:
            for copy in z_copies[i + 1]:
                copy.wait()
            begin(i + 1, 0)
            if i + 2 < sections:
                for copy in z_copies[i + 2]:
                    copy.start()
            if i >= 2:
                h_copies[i].start()
            if i + 2 == sections and i + 1 >= 2:
                h_copies[i + 1].start()
        if i == 1:
            own_hid.wait()
            get_w.wait()
            hidden_part()
            for copy in b_copies:
                copy.start()
            back_vm[j] = token_vm[j]
            weight_part(0)
        elif i >= 2:
            fetch(i - 1)
            h_copies[i - 1].wait_recv()
            weight_part(i - 1)
        arrive(i, last - 1)
        begin(i, last)
        if i == 0:
            own_dy.wait()
            arrive(0, last)
            fetch(0)
        elif i + 1 < sections:
            arrive(i, last)
    final = sections - 1
    arrive(final, last)
    fetch(final)
    h_copies[final].wait_recv()
    weight_part(final)
    for copy in b_copies:
        copy.wait()
    back_ref[...] = back_vm[...]
    for copies in stage.values():
        for copy in copies:
            copy.wait_send()
    for copy in h_copies[1:]:
        copy.wait_send()


def fused(dy, table, hid, blocks, w, sections, sources):
    tok, width = dy.shape
    held, slot_rows, hidden_width = hid.shape
    part_rows = blocks.shape[2]
    pairs = sources // 2
    any_space, vmem = pl.BlockSpec(memory_space=pl.ANY), pl.BlockSpec(memory_space=pltpu.VMEM)
    dma = pltpu.SemaphoreType.DMA
    f32, bf16 = jnp.float32, jnp.bfloat16
    back = (sources, 8, tok)
    flops = 2 * width * (2 * slot_rows * held * hidden_width + sections * sources * tok * part_rows)
    return pl.pallas_call(
        functools.partial(body, sections, sources),
        out_shape=(
            jax.ShapeDtypeStruct((sections, sources * tok, width), bf16),
            jax.ShapeDtypeStruct((part_rows, width), bf16),
            jax.ShapeDtypeStruct(hid.shape, bf16),
            jax.ShapeDtypeStruct(back, f32),
        ),
        in_specs=[any_space, vmem, vmem, vmem, any_space],
        out_specs=(any_space, vmem, vmem, vmem),
        scratch_shapes=[
            pltpu.VMEM((sections, sources) + table.shape, f32),
            pltpu.VMEM(blocks.shape, bf16),
            pltpu.VMEM((sources * tok, width), bf16),
            pltpu.VMEM(w.shape, bf16),
            pltpu.VMEM((part_rows, width), f32),
            pltpu.VMEM((part_rows, sources * tok), bf16),
            pltpu.VMEM((held, pairs, slot_rows // pairs, 2 * tok), bf16),
            pltpu.VMEM((slot_rows, TILE), bf16),
            pltpu.VMEM(hid.shape, f32),
            pltpu.VMEM(back, f32),
            pltpu.VMEM(back, f32),
            dma((4,)), dma((sections, 2)), dma((sections, 2)), dma((sections,)), dma((sections,)),
            dma((sections, 3, sources)), dma((sections, 3, sources)), dma((sources,)), dma((sources,)),
        ],
        compiler_params=pltpu.CompilerParams(
            collective_id=0, has_side_effects=True, vmem_limit_bytes=58 * 1024 * 1024),
        cost_estimate=pl.CostEstimate(
            flops=flops, bytes_accessed=2 * sections * sources * tok * width * 2, transcendentals=0),
    )(dy, table, hid, blocks, w)


def shards(d_output, gate_values, routes, hidden_saved, w_down):
    held, hidden_width, width = w_down.shape
    tok = d_output.shape[0]
    sources, capacity = hidden_saved.shape[2], hidden_saved.shape[3]
    sections = lax.axis_size("section")
    expert_count = held * sources
    f32 = jnp.float32

    match = routes[:, :, None] == jnp.arange(expert_count, dtype=jnp.int32)
    chosen = jnp.any(match, axis=1).astype(jnp.int32)
    rank = jnp.where(chosen > 0, jnp.cumsum(chosen, axis=0) - chosen, -1)
    gate = jnp.sum(jnp.where(match, gate_values[:, :, None].astype(f32), 0.0), axis=1)
    table = jnp.concatenate([rank.T.astype(f32), gate.T], axis=0)

    hid = hidden_saved.reshape(held, sources * capacity, hidden_width)
    blocks = hid.reshape(held, sources * capacity, sections, hidden_width // sections)
    blocks = jnp.transpose(blocks, (2, 1, 0, 3)).reshape(sections, sources * capacity, -1)
    _, d_weight, d_hidden, back = fused(d_output, table, hid, blocks, w_down, sections, sources)
    back = back[:, :held].reshape(expert_count, tok)
    d_gate = jnp.sum(jnp.where(match, back.T[:, None, :], 0.0), axis=2)
    return (
        d_hidden.reshape(hidden_saved.shape),
        d_weight.reshape(held, hidden_width // sections, width),
        d_gate,
    )


def solution(mesh):
    placed = (
        P(("section", "expert"), None),
        P(("section", "expert"), None),
        P(("section", "expert"), None),
        P("section", "expert", None, None, None),
        P("expert", None, None),
    )
    return jax.shard_map(
        shards,
        mesh=mesh,
        in_specs=placed,
        out_specs=(
            P("section", "expert", None, None, None),
            P("expert", "section", None),
            P(("section", "expert"), None),
        ),
        check_vma=False,
    )
```

time: 306 us -> 198 us (0.65)
  Pallas kernels: 0 us -> 176 us
  waiting for transfers between devices: 156 us -> 0 us
  blocking collectives: 78.3 us -> 0 us
  matrix products: 36.9 us -> 0 us
  between operations: 14.2 us -> 0.67 us
  local copies, waits for them, and re-layouts: 7.35 us -> 17.6 us
  starting transfers between devices: 7.91 us -> 0 us
    pallas_call x0 -> x1, Pallas kernels: none -> 176 us  [fused(): pl.pallas_call(functools.partial(body, sections, sources), out_shape=(jax...]
    all_gather x2 -> x0, waiting for transfers between devices: 155 us -> none  [the longest x1 85.1 us: shards(): by_section = lax.all_gather(d_output, 'section')]
    all_gather x1 -> x0, blocking collectives: 78.3 us -> none  [shards(): table = lax.all_gather(table, ('section', 'expert'))]
    dot_general x3 -> x0, matrix products: 36.9 us -> none  [the longest x1 19.2 us: shards(): jnp.einsum('sjtef,sjtd->efd', scattered, dy, preferred_element_type=f32)]
    all_to_all x2 -> x0, starting transfers between devices: 7.84 us -> none  [the longest x1 3.92 us: shards(): lax.all_to_all(token_value, 'expert', split_axis=0, concat_axis=0, tiled=...]
    unnamed x6, local copies, waits for them, and re-layouts: 0.01 us -> 4.47 us
    reshape x0 -> x1, local copies, waits for them, and re-layouts: none -> 3.9 us  [shards(): jnp.transpose(blocks, (2, 1, 0, 3))]
  transfers between devices with their start and end apart: 4 -> 0, of which waited for: 2 -> 0; matrix products, arithmetic and copies ran while one was open for 10% -> 0% of each run, Pallas kernels for 0% -> 0%
where the time goes in v2:
time: 198 us
  Pallas kernels  176 us (89%)
  local copies, waits for them, and re-layouts  17.6 us (9%)
  other arithmetic  3.51 us (2%)
    pallas_call x1, Pallas kernels, fused(): pl.pallas_call(functools.partial(body, sections, sources), out_shape=(jax...  176 us
    another operation x1, local copies, waits for them, and re-layouts, shards(): hid.reshape(held, sources * capacity, sections, hidden_width // sections)  4.75 us
    unnamed x6, local copies, waits for them, and re-layouts  4.47 us

profile of v2, /device:TPU:0, one launch (start us, length us, event | category | flops | bytes accessed | tf_op | source)
XLA Modules:
  0.0 197.5 jit_solution(11008731581262316363)
XLA Ops:
  0.6 0.7 fusion
  1.3 0.7 convert_element_type.18
  2.0 0.7 select_reduce_fusion.1
  2.7 0.1 copy.21
  2.8 0.2 reduce_window_sum.11
  3.0 0.1 copy.22
  3.1 0.6 pad_maximum_fusion.tab_ref
  3.7 4.8 %reshape_reshape.3 = bf16[2,576,4,192]{3,2,1,0:T(4,128)(2,1)S(1)} reshape(bf16[1,2,8,72,768]{4,3,2,1,0:T(8,128)(2,1)} %param.8) | data formatting | bytes 3538944 | tf_op jit(solution)/shard_map/reshape;reshape | solution.py:302
  8.5 3.4 %copy.23 = bf16[4,576,2,192]{1,3,2,0:T(8,128)(2,1)} copy(bf16[4,576,2,192]{3,0,1,2:T(4,128)(2,1)S(1)} %bitcast.13) | data formatting | bytes 3538944 | tf_op jit(solution)/shard_map/transpose | solution.py:303
  11.9 3.9 %copy.24.blocks_ref = bf16[4,576,384]{2,1,0:T(8,128)(2,1)} copy(bf16[4,576,384]{1,2,0:T(8,128)(2,1)} %bitcast.14) | data formatting | bytes 3538944 | tf_op jit(solution)/shard_map/reshape | solution.py:303
  15.8 0.0 copy-start.1
  15.8 175.7 %shard_map.76 = (bf16[4,1024,4096]{2,1,0:T(8,128)(2,1)}, bf16[384,4096]{1,0:T(8,128)(2,1)}, bf16[2,576,768]{2,1,0:T(8,128)(2,1)}, f32[8,8,128]{2,1,0:T(8,128)}) custom-call(bf16[128,4096]{1,0:T(8,128)(2,1)} %dy_ref.1, f32[32,128]{1,0:T(8,128)} %pad_maximum_fusion.tab_ref, bf16[2,576,768]{2,1,0:T(8,128)(2,1)} %bitcast.17, ...), custom_call_target="tpu_custom_call" | custom-call | flops 27380416512 | bytes 67108864 | tf_op jit(solution)/shard_map/pallas_call | solution.py:255
  191.5 0.0 copy-start
  191.5 0.9 slice.3
  192.4 0.0 copy-done.1
  192.4 0.6 select_reduce_fusion
  193.0 2.8 %copy.27 = bf16[1,2,8,72,768]{4,3,2,1,0:T(8,128)(2,1)} copy(bf16[1,2,8,72,768]{4,3,2,1,0:T(8,128)(2,1)} %bitcast.16) | data formatting | bytes 3538944
  195.8 0.0 copy-done
  195.8 1.7 copy.28
  (2 shorter events, 0.0 us)
Async XLA Ops:
  15.8 176.6 %copy-start.1 = (s32[128,8]{0,1:T(8,128)S(1)}, s32[128,8]{0,1:T(8,128)}, u32[]{:S(2)}) copy-start(s32[128,8]{0,1:T(8,128)} %param.7) | copy-start | bytes 12292
  191.5 4.3 %copy-start = (bf16[384,4096]{1,0:T(8,128)(2,1)S(1)}, bf16[384,4096]{1,0:T(8,128)(2,1)}, u32[]{:S(2)}) copy-start(bf16[384,4096]{1,0:T(8,128)(2,1)} %get-tuple-element.7) | copy-start | bytes 9437188

commit v3 on v2

--- a/solution.py
+++ b/solution.py
@@ -21,9 +21,9 @@
     return lax.dot_general(a, b, (dims, ((), ())), preferred_element_type=jnp.float32)
 
 
-def body(sections, sources, dy_ref, tab_ref, hid_ref, blocks_ref, w_ref,
-         all_ref, dw_ref, dh_ref, back_ref,
-         tabs, parts, dy_vm, w_vm, acc, scattered, picked, rows_vm, plain, token_vm, back_vm,
+def body(sections, sources, dy_ref, route_ref, gates_ref, hid_ref, w_ref,
+         all_ref, dw_ref, dh_ref, dg_ref,
+         tabs, blocks_ref, parts, dy_vm, w_vm, acc, scattered, picked, rows_vm, plain, token_vm, back_vm,
          local_sem, z_send, z_recv, h_send, h_recv, e_send, e_recv, b_send, b_recv):
     f32, bf16 = jnp.float32, jnp.bfloat16
     z, j = lax.axis_index("section"), lax.axis_index("expert")
@@ -32,8 +32,8 @@
     pairs = sources // 2
     pair_rows = slot_rows // pairs
     capacity = pair_rows // 2
-    part_width = blocks_ref.shape[2] // held
-    expert_count = tab_ref.shape[0] // 2
+    part_width = hidden_width // sections
+    expert_count = held * sources
     half_rows = tok // 2
     bits = [1 << b for b in range(sources.bit_length() - 1)]
     orders = (bits[1:] + bits[:1], bits[1:][::-1] + bits[:1])
@@ -44,7 +44,19 @@
     def section_at(i):
         return (z + sections - steps[i]) % sections
 
-    tabs[z, j] = tab_ref[...]
+    expert_row = lax.broadcasted_iota(jnp.int32, (expert_count, tok), 0)
+    named = jnp.zeros((expert_count, tok), f32)
+    gate = jnp.zeros((expert_count, tok), f32)
+    for k in range(route_ref.shape[0]):
+        match = expert_row == route_ref[k:k + 1, :]
+        named = named + jnp.where(match, 1.0, 0.0)
+        gate = gate + jnp.where(match, gates_ref[k:k + 1, :], 0.0)
+    before = jnp.where(
+        lax.broadcasted_iota(jnp.int32, (tok, tok), 0) < lax.broadcasted_iota(jnp.int32, (tok, tok), 1),
+        1.0, 0.0).astype(bf16)
+    rank = dot(named.astype(bf16), before, ((1,), (0,)))
+    tabs[z, j, :expert_count] = jnp.where(named > 0, rank, -1.0)
+    tabs[z, j, expert_count:] = gate
     barrier = pltpu.get_barrier_semaphore()
     for d in range(1, sections):
         pl.semaphore_signal(barrier, inc=1, device_id=((z + d) % sections, j), device_id_type=MESH)
@@ -53,7 +65,6 @@
     pl.semaphore_wait(barrier, sections + sources - 2)
 
     own_dy = pltpu.make_async_copy(dy_ref, all_ref.at[z, pl.ds(pl.multiple_of(j * tok, tok), tok)], local_sem.at[0])
-    own_hid = pltpu.make_async_copy(blocks_ref.at[z], parts.at[z], local_sem.at[1])
     get_w = pltpu.make_async_copy(w_ref, w_vm, local_sem.at[2])
 
     def remote(source, target, send, recv, to):
@@ -186,12 +197,17 @@
     token_vm[...] = jnp.zeros(token_vm.shape, f32)
     begin(0, 0)
     own_dy.start()
-    own_hid.start()
     get_w.start()
     if sections > 1:
         for copy in z_copies[1]:
             copy.start()
+    for s in range(sections):
+        for e in range(held):
+            blocks_ref[s, :, e * part_width:(e + 1) * part_width] = (
+                hid_ref[e, :, s * part_width:(s + 1) * part_width])
+    if sections > 1:
         h_copies[1].start()
+    parts[z] = blocks_ref[z]
     for i in range(sections):
         for k in range(1, last):
             arrive(i, k - 1)
@@ -208,7 +224,6 @@
             if i + 2 == sections and i + 1 >= 2:
                 h_copies[i + 1].start()
         if i == 1:
-            own_hid.wait()
             get_w.wait()
             hidden_part()
             for copy in b_copies:
@@ -234,7 +249,11 @@
     weight_part(final)
     for copy in b_copies:
         copy.wait()
-    back_ref[...] = back_vm[...]
+    routed = jnp.zeros(route_ref.shape, f32)
+    for e in range(expert_count):
+        value = back_vm[e // held, e % held:e % held + 1, :]
+        routed = routed + jnp.where(route_ref[...] == e, value, 0.0)
+    dg_ref[...] = routed
     for copies in stage.values():
         for copy in copies:
             copy.wait_send()
@@ -242,10 +261,11 @@
         copy.wait_send()
 
 
-def fused(dy, table, hid, blocks, w, sections, sources):
+def fused(dy, routes, gates, hid, w, sections, sources):
     tok, width = dy.shape
     held, slot_rows, hidden_width = hid.shape
-    part_rows = blocks.shape[2]
+    part_rows = held * hidden_width // sections
+    blocks = (sections, slot_rows, part_rows)
     pairs = sources // 2
     any_space, vmem = pl.BlockSpec(memory_space=pl.ANY), pl.BlockSpec(memory_space=pltpu.VMEM)
     dma = pltpu.SemaphoreType.DMA
@@ -258,13 +278,14 @@
             jax.ShapeDtypeStruct((sections, sources * tok, width), bf16),
             jax.ShapeDtypeStruct((part_rows, width), bf16),
             jax.ShapeDtypeStruct(hid.shape, bf16),
-            jax.ShapeDtypeStruct(back, f32),
+            jax.ShapeDtypeStruct(routes.shape, f32),
         ),
         in_specs=[any_space, vmem, vmem, vmem, any_space],
         out_specs=(any_space, vmem, vmem, vmem),
         scratch_shapes=[
-            pltpu.VMEM((sections, sources) + table.shape, f32),
-            pltpu.VMEM(blocks.shape, bf16),
+            pltpu.VMEM((sections, sources, 2 * held * sources, tok), f32),
+            pltpu.VMEM(blocks, bf16),
+            pltpu.VMEM(blocks, bf16),
             pltpu.VMEM((sources * tok, width), bf16),
             pltpu.VMEM(w.shape, bf16),
             pltpu.VMEM((part_rows, width), f32),
@@ -281,7 +302,7 @@
             collective_id=0, has_side_effects=True, vmem_limit_bytes=58 * 1024 * 1024),
         cost_estimate=pl.CostEstimate(
             flops=flops, bytes_accessed=2 * sections * sources * tok * width * 2, transcendentals=0),
-    )(dy, table, hid, blocks, w)
+    )(dy, routes, gates, hid, w)
 
 
 def shards(d_output, gate_values, routes, hidden_saved, w_down):
@@ -289,25 +310,13 @@
     tok = d_output.shape[0]
     sources, capacity = hidden_saved.shape[2], hidden_saved.shape[3]
     sections = lax.axis_size("section")
-    expert_count = held * sources
-    f32 = jnp.float32
-
-    match = routes[:, :, None] == jnp.arange(expert_count, dtype=jnp.int32)
-    chosen = jnp.any(match, axis=1).astype(jnp.int32)
-    rank = jnp.where(chosen > 0, jnp.cumsum(chosen, axis=0) - chosen, -1)
-    gate = jnp.sum(jnp.where(match, gate_values[:, :, None].astype(f32), 0.0), axis=1)
-    table = jnp.concatenate([rank.T.astype(f32), gate.T], axis=0)
-
     hid = hidden_saved.reshape(held, sources * capacity, hidden_width)
-    blocks = hid.reshape(held, sources * capacity, sections, hidden_width // sections)
-    blocks = jnp.transpose(blocks, (2, 1, 0, 3)).reshape(sections, sources * capacity, -1)
-    _, d_weight, d_hidden, back = fused(d_output, table, hid, blocks, w_down, sections, sources)
-    back = back[:, :held].reshape(expert_count, tok)
-    d_gate = jnp.sum(jnp.where(match, back.T[:, None, :], 0.0), axis=2)
+    _, d_weight, d_hidden, d_gate = fused(
+        d_output, routes.T, gate_values.T.astype(jnp.float32), hid, w_down, sections, sources)
     return (
         d_hidden.reshape(hidden_saved.shape),
         d_weight.reshape(held, hidden_width // sections, width),
-        d_gate,
+        d_gate.T,
     )
 
 

time: 198 us -> 183 us (0.924)
  local copies, waits for them, and re-layouts: 17.6 us -> 5.21 us
  other arithmetic: 3.51 us -> 1.28 us
    another operation x2 -> x0, local copies, waits for them, and re-layouts: 4.8 us -> none  [the longest x1 4.75 us: shards(): hid.reshape(held, sources * capacity, sections, hidden_width // sections)]
    reshape x1 -> x0, local copies, waits for them, and re-layouts: 3.9 us -> none  [shards(): jnp.transpose(blocks, (2, 1, 0, 3))]
    transpose x1 -> x0, local copies, waits for them, and re-layouts: 3.44 us -> none  [shards(): jnp.transpose(blocks, (2, 1, 0, 3))]
    unnamed x6 -> x7, local copies, waits for them, and re-layouts: 4.47 us -> 5.21 us
where the time goes in v3:
time: 183 us; the launch traced here: 182 us
  Pallas kernels  175 us (96%)
  local copies, waits for them, and re-layouts  5.21 us (3%)
    pallas_call x1, Pallas kernels, fused(): pl.pallas_call(functools.partial(body, sections, sources), out_shape=(jax...  175 us
    unnamed x7, local copies, waits for them, and re-layouts  5.21 us

profile of v3, /device:TPU:0, one launch (start us, length us, event | category | flops | bytes accessed | tf_op | source)
XLA Modules:
  0.0 182.4 jit_solution(7750712691297084895)
XLA Ops:
  0.6 1.3 convert_bitcast_fusion.gates_ref
  1.9 175.3 %shard_map.76 = (bf16[4,1024,4096]{2,1,0:T(8,128)(2,1)}, bf16[384,4096]{1,0:T(8,128)(2,1)}, bf16[2,576,768]{2,1,0:T(8,128)(2,1)}, f32[8,128]{1,0:T(8,128)}) custom-call(bf16[128,4096]{1,0:T(8,128)(2,1)} %dy_ref.1, s32[8,128]{1,0:T(8,128)} %bitcast.11, f32[8,128]{1,0:T(8,128)} %convert_bitcast_fusion.gates_ref, bf16[2,576,768]{2,1,0:T(8,128)(2,1)} %bitcast.10, ...), custom_call_target="tpu_custom_call" | custom-call | flops 27380416512 | bytes 67108864 | tf_op jit(solution)/shard_map/pallas_call | solution.py:275
  177.2 0.0 copy-start
  177.2 2.9 %copy.11 = bf16[1,2,8,72,768]{4,3,2,1,0:T(8,128)(2,1)} copy(bf16[1,2,8,72,768]{4,3,2,1,0:T(8,128)(2,1)} %bitcast.8) | data formatting | bytes 3538944
  180.2 0.0 copy-done
  180.2 0.0 copy-start.1
  180.2 1.7 copy.12
  181.8 0.0 copy-done.1
  181.8 0.6 copy.13
Async XLA Ops:
  177.2 3.0 %copy-start = (bf16[384,4096]{1,0:T(8,128)(2,1)S(1)}, bf16[384,4096]{1,0:T(8,128)(2,1)}, u32[]{:S(2)}) copy-start(bf16[384,4096]{1,0:T(8,128)(2,1)} %get-tuple-element.7) | copy-start | bytes 9437188
  180.2 1.7 copy-start.1

commit v4 on v1

v4 whole, which is shorter than its diff:
```python
import functools

import jax
import jax.numpy as jnp
from jax import lax
from jax.experimental import pallas as pl
from jax.experimental.pallas import tpu as pltpu
from jax.sharding import PartitionSpec as P

MESH = pl.DeviceIdType.MESH
TILE = 512


def flipped(index, bits):
    for bit in bits:
        index = index + bit * (1 - 2 * ((index // bit) % 2))
    return index


def dot(a, b, dims):
    return lax.dot_general(a, b, (dims, ((), ())), preferred_element_type=jnp.float32)


def body(sections, sources, dy_ref, route_ref, gates_ref, hid_ref, w_ref,
         tok_ref, dw_ref, dh_ref, dg_ref,
         tabs, blocks_ref, parts, dy_vm, w_vm, acc, near, scattered, picked, rows_vm, plain,
         partner_rows, token_vm, back_vm,
         local_sem, fetch_sem, own_send, own_recv, z_send, z_recv, s_send, s_recv, h_send, h_recv,
         x_send, x_recv, o_send, o_recv, b_send, b_recv):
    f32, bf16 = jnp.float32, jnp.bfloat16
    z, j = lax.axis_index("section"), lax.axis_index("expert")
    tok, width = dy_ref.shape
    held, slot_rows, hidden_width = hid_ref.shape
    pairs = sources // 2
    pair_rows = slot_rows // pairs
    capacity = pair_rows // 2
    part_width = hidden_width // sections
    part_rows = held * part_width
    expert_count = held * sources
    half_rows = tok // 2
    chunks = tok_ref.shape[0]
    hops = sections - 1
    q = (j % 2) * pairs + j // 2
    bits = [1 << b for b in range(sources.bit_length() - 1)]
    orders = (bits, bits[:-1][::-1] + bits[-1:])
    half = q % 2

    def index_of(place):
        return (place % pairs) * 2 + place // pairs

    def device(place):
        return (z, index_of(place))

    def rows_at(place, start, count):
        return pl.ds(pl.multiple_of(place * tok + start, 16), count)

    def columns(k):
        return pl.ds(pl.multiple_of(half * (width // 2) + k * TILE, TILE), TILE)

    def remote(source, target, send, recv, to):
        return pltpu.make_async_remote_copy(
            source, target, send, recv, device_id=to, device_id_type=MESH)

    expert_row = lax.broadcasted_iota(jnp.int32, (expert_count, tok), 0)
    named = jnp.zeros((expert_count, tok), f32)
    gate = jnp.zeros((expert_count, tok), f32)
    for k in range(route_ref.shape[0]):
        match = expert_row == route_ref[k:k + 1, :]
        named = named + jnp.where(match, 1.0, 0.0)
        gate = gate + jnp.where(match, gates_ref[k:k + 1, :], 0.0)
    before = jnp.where(
        lax.broadcasted_iota(jnp.int32, (tok, tok), 0) < lax.broadcasted_iota(jnp.int32, (tok, tok), 1),
        1.0, 0.0).astype(bf16)
    rank = dot(named.astype(bf16), before, ((1,), (0,)))
    tabs[z, q, :expert_count] = jnp.where(named > 0, rank, -1.0)
    tabs[z, q, expert_count:] = gate

    barrier = pltpu.get_barrier_semaphore()
    for d in range(1, sections):
        pl.semaphore_signal(barrier, inc=1, device_id=((z + d) % sections, j), device_id_type=MESH)
    for r in range(1, sources):
        pl.semaphore_signal(barrier, inc=1, device_id=(z, (j + r) % sources), device_id_type=MESH)
    pl.semaphore_wait(barrier, sections + sources - 2)

    own_dy = pltpu.make_async_copy(dy_ref, dy_vm.at[rows_at(q, 0, tok)], local_sem.at[0])

    def get_w(e):
        return pltpu.make_async_copy(w_ref.at[e], w_vm, local_sem.at[1])


    own = []

    def begin(k):
        made = []
        for part in range(3):
            order = orders[part % 2]
            have = [[]]
            for bit in order[:k]:
                have = have + [r + [bit] for r in have]
            to = device(flipped(q, [order[k]]))
            for r in have:
                place = flipped(q, r)
                slot = sum(r) + order[k]
                sems = own_send.at[part, slot], own_recv.at[part, slot]
                if part == 2:
                    copy = remote(tabs.at[z, place], tabs.at[z, place], *sems, to)
                else:
                    target = dy_vm.at[rows_at(place, part * half_rows, half_rows)]
                    source = target if r else dy_ref.at[pl.ds(part * half_rows, half_rows)]
                    copy = remote(source, target, *sems, to)
                copy.start()
                made.append(copy)
        own.append(made)

    def arrive(k):
        for copy in own[k]:
            copy.wait_recv()

    def present(way, r):
        return z >= r + 1 if way == 0 else z + r + 1 < sections

    def z_valid(way, r):
        if way == 0:
            return jnp.logical_and(z >= r, z + 1 < sections)
        return jnp.logical_and(z + r < sections, z >= 1)

    def z_copies(k, way, r):
        s = (z - r + sections if way == 0 else z + r) % sections
        to = ((z + 1 if way == 0 else z - 1 + sections) % sections, j)
        low = q // 2 * 2
        target = tok_ref.at[k, s, rows_at(low, 0, 2 * tok)]
        source = dy_vm.at[rows_at(low, 0, 2 * tok), columns(k)] if r == 0 else target
        made = [remote(source, target, z_send.at[k, way, r], z_recv.at[k, way, r], to)]
        if k == 0:
            table = tabs.at[s, pl.ds(low, 2)]
            made.append(remote(
                table, table, z_send.at[chunks, way, r], z_recv.at[chunks, way, r], to))
        return made

    def plane_copies(k, way, r, b):
        s = (z - 1 - r + sections if way == 0 else z + 1 + r) % sections
        bit = bits[b]
        to = device(flipped(q, [bit]))
        low = q // bit * bit
        target = tok_ref.at[k, s, rows_at(low, 0, bit * tok)]
        made = [remote(target, target, s_send.at[k, way, r, b], s_recv.at[k, way, r, b], to)]
        if k == 0:
            table = tabs.at[s, pl.ds(low, bit)]
            made.append(remote(
                table, table, s_send.at[chunks, way, r, b], s_recv.at[chunks, way, r, b], to))
        return made

    def each_way(condition, r, work):
        for way in range(2):
            @pl.when(condition(way, r))
            def _():
                work(way)

    def start_all(copies):
        for copy in copies:
            copy.start()

    def wait_in(copies):
        for copy in copies:
            copy.wait_recv()

    def wait_out(copies):
        for copy in copies:
            copy.wait_send()

    h_copies, x_copies, fetches = [None], [], [None]
    mate = device(flipped(q, [1]))
    for i in range(sections):
        to = (z + i) % sections
        if i:
            h_copies.append(remote(
                blocks_ref.at[to], parts.at[0, z], h_send.at[i], h_recv.at[i], (to, j)))
        source = (z - i + sections) % sections
        x_copies.append(remote(
            parts.at[0, source], parts.at[1, source], x_send.at[i], x_recv.at[i], mate))

    def row_of(s, p, row):
        return jnp.concatenate(
            [tabs[s, p, pl.ds(row, 1), :], tabs[s, pairs + p, pl.ds(row, 1), :]], axis=1)

    def gate_row(s, p, expert):
        return row_of(s, p, expert_count + expert)

    def chosen(s, p, expert):
        rank = row_of(s, p, expert)
        lane = lax.broadcasted_iota(jnp.int32, rank.shape, 1)
        rank = jnp.where(rank < 0, -1.0, rank + jnp.where(lane < tok, 0.0, float(capacity)))
        place = lax.broadcasted_iota(jnp.int32, (pair_rows, 2 * tok), 0).astype(f32)
        return place == rank

    def scatter_part():
        mate_index = index_of(flipped(q, [1]))

        def one(i, _):
            s = (z + i) % sections
            for o, first in ((0, j * held), (1, mate_index * held)):
                for p in range(pairs):
                    hid = parts[o, s, p * pair_rows:(p + 1) * pair_rows, :]
                    for e in range(held):
                        gates = jnp.where(
                            chosen(s, p, first + e), gate_row(s, p, first + e), 0.0).astype(bf16)
                        rows = slice(e * part_width, (e + 1) * part_width)
                        moved = dot(hid, gates, ((0,), (0,)))[rows].astype(bf16)
                        at = o * part_rows + e * part_width
                        for c in range(2):
                            start = pl.multiple_of(i * (sources * tok) + (c * pairs + p) * tok, tok)
                            scattered[at:at + part_width, pl.ds(start, tok)] = (
                                moved[:, c * tok:(c + 1) * tok])
            return 0

        lax.fori_loop(0, sections, one, 0)

    o_copies = []

    def weight_chunk(k):
        def fetch(i):
            return pltpu.make_async_copy(
                tok_ref.at[k, (z + i) % sections], near.at[i % 2], fetch_sem.at[i % 2])

        if sections > 1:
            fetch(1).start()
        acc[...] = dot(scattered[:, :sources * tok], dy_vm[:, columns(k)], ((1,), (0,)))

        def one(i, _):
            fetch(i).wait()

            @pl.when(i + 1 < sections)
            def _():
                fetch(i + 1).start()

            start = pl.multiple_of(i * (sources * tok), tok)
            acc[...] += dot(
                scattered[:, pl.ds(start, sources * tok)], near[i % 2], ((1,), (0,)))
            return 0

        lax.fori_loop(1, sections, one, 0)
        partner_rows[k] = acc[part_rows:].astype(bf16)
        copy = remote(
            partner_rows.at[k], dw_ref.at[:, columns(k)], o_send.at[k], o_recv.at[k], mate)
        copy.start()
        o_copies.append(copy)
        dw_ref[:, columns(k)] = acc[:part_rows].astype(bf16)

    b_copies = []
    for r in range(1, sources):
        to = (j + r) % sources
        b_copies.append(remote(token_vm.at[to], back_vm.at[j], b_send.at[r], b_recv.at[r], (z, to)))

    def hidden_tiles(e, first, count):
        def tile(t, _):
            cols = pl.ds(pl.multiple_of(t * TILE, TILE), TILE)
            for p in range(pairs):
                tokens = jnp.concatenate(
                    [dy_vm[p * tok:(p + 1) * tok, cols],
                     dy_vm[(pairs + p) * tok:(pairs + p + 1) * tok, cols]], axis=0)
                rows_vm[p * pair_rows:(p + 1) * pair_rows, :] = dot(
                    picked[e, p], tokens, ((1,), (0,))).astype(bf16)
            plain[...] += dot(rows_vm[...], w_vm[:, cols], ((1,), (1,)))
            return 0

        lax.fori_loop(first, first + count, tile, 0)

    def hidden_start():
        for e in range(held):
            for p in range(pairs):
                picked[e, p] = jnp.where(chosen(z, p, j * held + e), 1.0, 0.0).astype(bf16)

    def hidden_next(e):
        if e:
            get_w(e).start()
        plain[...] = jnp.zeros(plain.shape, f32)
        get_w(e).wait()

    def hidden_done(e):
        for p in range(pairs):
            rows = slice(p * pair_rows, (p + 1) * pair_rows)
            here = chosen(z, p, j * held + e)
            gate = jnp.sum(
                jnp.where(here, gate_row(z, p, j * held + e), 0.0), axis=1, keepdims=True)
            value = plain[rows, :]
            dh_ref[e, rows, :] = (value * gate).astype(bf16)
            total = jnp.sum(value * hid_ref[e, rows, :].astype(f32), axis=1, keepdims=True)
            by_token = jnp.sum(jnp.where(here, total, 0.0), axis=0, keepdims=True)
            token_vm[2 * p, e:e + 1, :] = by_token[:, :tok]
            token_vm[2 * p + 1, e:e + 1, :] = by_token[:, tok:]

    def hidden_end():
        for copy in b_copies:
            copy.start()
        back_vm[j] = token_vm[j]

    tiles = width // TILE
    step = max(1, tiles // 4)
    work = [hidden_start]
    for e in range(held):
        work.append(functools.partial(hidden_next, e))
        for first in range(0, tiles, step):
            work.append(functools.partial(hidden_tiles, e, first, min(step, tiles - first)))
        work.append(functools.partial(hidden_done, e))
    work.append(hidden_end)

    def some(count):
        for _ in range(count):
            if work:
                work.pop(0)()

    last = len(bits) - 1
    begin(0)
    own_dy.start()
    get_w(0).start()
    for s in range(sections):
        for e in range(held):
            blocks_ref[s, :, e * part_width:(e + 1) * part_width] = (
                hid_ref[e, :, s * part_width:(s + 1) * part_width])
    start_all(h_copies[1:])
    parts[0, z] = blocks_ref[z]
    token_vm[...] = jnp.zeros(token_vm.shape, f32)
    for k in range(1, last):
        arrive(k - 1)
        begin(k)
    x_copies[0].start()
    own_dy.wait()
    arrive(last - 1)
    for k in range(chunks):
        each_way(z_valid, 0, lambda way: start_all(z_copies(k, way, 0)))
    begin(last)
    for i in range(1, sections):
        h_copies[i].wait_recv()
        x_copies[i].start()
    arrive(last)
    some(1)
    units = [(k, r) for k in range(chunks) for r in range(hops)]
    built = False
    for t in range(len(units) + last):
        if t < len(units):
            k, r = units[t]

            def forward(way):
                wait_in(z_copies(k, way, r))
                start_all(plane_copies(k, way, r, 1))

            each_way(present, r, forward)
            if r + 1 < hops:
                each_way(z_valid, r + 1, lambda way: start_all(z_copies(k, way, r + 1)))
        for b in range(1, last + 1):
            if 0 <= t - b < len(units):
                k, r = units[t - b]

                def pass_on(way):
                    wait_in(plane_copies(k, way, r, b))
                    if b < last:
                        start_all(plane_copies(k, way, r, b + 1))

                each_way(present, r, pass_on)
        some(2)
        if t >= last and (t - last + 1) % hops == 0:
            if not built:
                for copy in x_copies:
                    copy.wait_recv()
                scatter_part()
                built = True
            weight_chunk((t - last) // hops)
    some(len(work))
    for copy in b_copies:
        copy.wait()
    routed = jnp.zeros(route_ref.shape, f32)
    for e in range(expert_count):
        value = back_vm[e // held, e % held:e % held + 1, :]
        routed = routed + jnp.where(route_ref[...] == e, value, 0.0)
    dg_ref[...] = routed
    for copies in own:
        wait_out(copies)
    wait_out(h_copies[1:])
    wait_out(x_copies)
    for k, r in units:
        each_way(z_valid, r, lambda way: wait_out(z_copies(k, way, r)))
        for b in range(1, last + 1):
            each_way(present, r, lambda way: wait_out(plane_copies(k, way, r, b)))
    for copy in o_copies:
        copy.wait()


def fused(dy, routes, gates, hid, w, sections, sources):
    tok, width = dy.shape
    held, slot_rows, hidden_width = hid.shape
    part_rows = held * hidden_width // sections
    blocks = (sections, slot_rows, part_rows)
    pairs = sources // 2
    chunks = width // 2 // TILE
    stages = sources.bit_length() - 1
    any_space, vmem = pl.BlockSpec(memory_space=pl.ANY), pl.BlockSpec(memory_space=pltpu.VMEM)
    dma = pltpu.SemaphoreType.DMA
    f32, bf16 = jnp.float32, jnp.bfloat16
    back = (sources, 8, tok)
    flops = 2 * width * (2 * slot_rows * held * hidden_width + sections * sources * tok * part_rows)
    hops = max(1, sections - 1)
    return pl.pallas_call(
        functools.partial(body, sections, sources),
        out_shape=(
            jax.ShapeDtypeStruct((chunks, sections, sources * tok, TILE), bf16),
            jax.ShapeDtypeStruct((part_rows, width), bf16),
            jax.ShapeDtypeStruct(hid.shape, bf16),
            jax.ShapeDtypeStruct(routes.shape, f32),
        ),
        in_specs=[any_space, vmem, vmem, vmem, any_space],
        out_specs=(any_space, vmem, vmem, vmem),
        scratch_shapes=[
            pltpu.VMEM((sections, sources, 2 * held * sources, tok), f32),
            pltpu.VMEM(blocks, bf16),
            pltpu.VMEM((2,) + blocks, bf16),
            pltpu.VMEM((sources * tok, width), bf16),
            pltpu.VMEM(w.shape[1:], bf16),
            pltpu.VMEM((2 * part_rows, TILE), f32),
            pltpu.VMEM((2, sources * tok, TILE), bf16),
            pltpu.VMEM((2 * part_rows, sections * sources * tok), bf16),
            pltpu.VMEM((held, pairs, slot_rows // pairs, 2 * tok), bf16),
            pltpu.VMEM((slot_rows, TILE), bf16),
            pltpu.VMEM(hid.shape[1:], f32),
            pltpu.VMEM((chunks, part_rows, TILE), bf16),
            pltpu.VMEM(back, f32),
            pltpu.VMEM(back, f32),
            dma((2,)), dma((2,)), dma((3, sources)), dma((3, sources)),
            dma((chunks + 1, 2, hops)), dma((chunks + 1, 2, hops)),
            dma((chunks + 1, 2, hops, stages)), dma((chunks + 1, 2, hops, stages)),
            dma((sections,)), dma((sections,)), dma((sections,)), dma((sections,)),
            dma((chunks,)), dma((chunks,)), dma((sources,)), dma((sources,)),
        ],
        compiler_params=pltpu.CompilerParams(
            collective_id=0, has_side_effects=True, vmem_limit_bytes=60 * 1024 * 1024),
        cost_estimate=pl.CostEstimate(
            flops=flops, bytes_accessed=sections * sources * tok * width * 2, transcendentals=0),
    )(dy, routes, gates, hid, w)


def shards(d_output, gate_values, routes, hidden_saved, w_down):
    held, hidden_width, width = w_down.shape
    tok = d_output.shape[0]
    sources, capacity = hidden_saved.shape[2], hidden_saved.shape[3]
    sections = lax.axis_size("section")
    hid = hidden_saved.reshape(held, sources * capacity, hidden_width)
    _, d_weight, d_hidden, d_gate = fused(
        d_output, routes.T, gate_values.T.astype(jnp.float32), hid, w_down, sections, sources)
    return (
        d_hidden.reshape(hidden_saved.shape),
        d_weight.reshape(held, hidden_width // sections, width),
        d_gate.T,
    )


def solution(mesh):
    placed = (
        P(("section", "expert"), None),
        P(("section", "expert"), None),
        P(("section", "expert"), None),
        P("section", "expert", None, None, None),
        P("expert", None, None),
    )
    return jax.shard_map(
        shards,
        mesh=mesh,
        in_specs=placed,
        out_specs=(
            P("section", "expert", None, None, None),
            P("expert", "section", None),
            P(("section", "expert"), None),
        ),
        check_vma=False,
    )
```

time: 306 us -> 180 us (0.59)
  Pallas kernels: 0 us -> 172 us
  waiting for transfers between devices: 156 us -> 0 us
  blocking collectives: 78.3 us -> 0 us
  matrix products: 36.9 us -> 0 us
  between operations: 14.2 us -> 0.65 us
  starting transfers between devices: 7.91 us -> 0 us
  other arithmetic: 4.89 us -> 1.28 us
    pallas_call x0 -> x1, Pallas kernels: none -> 172 us  [fused(): pl.pallas_call(functools.partial(body, sections, sources), out_shape=(jax...]
    all_gather x2 -> x0, waiting for transfers between devices: 155 us -> none  [the longest x1 85.1 us: shards(): by_section = lax.all_gather(d_output, 'section')]
    all_gather x1 -> x0, blocking collectives: 78.3 us -> none  [shards(): table = lax.all_gather(table, ('section', 'expert'))]
    dot_general x3 -> x0, matrix products: 36.9 us -> none  [the longest x1 19.2 us: shards(): jnp.einsum('sjtef,sjtd->efd', scattered, dy, preferred_element_type=f32)]
    all_to_all x2 -> x0, starting transfers between devices: 7.84 us -> none  [the longest x1 3.92 us: shards(): lax.all_to_all(token_value, 'expert', split_axis=0, concat_axis=0, tiled=...]
    unnamed x6 -> x7, local copies, waits for them, and re-layouts: 0.01 us -> 5.21 us
    another operation x2 -> x0, local copies, waits for them, and re-layouts: 4.82 us -> none  [the longest x1 4.76 us: shards(): blocks = hidden_saved[0].reshape(held, sources, capacity, sections, -1)]
  transfers between devices with their start and end apart: 4 -> 0, of which waited for: 2 -> 0; matrix products, arithmetic and copies ran while one was open for 10% -> 0% of each run, Pallas kernels for 0% -> 0%
where the time goes in v4:
time: 180 us; the launch traced here: 179 us
  Pallas kernels  172 us (96%)
  local copies, waits for them, and re-layouts  5.21 us (3%)
    pallas_call x1, Pallas kernels, fused(): pl.pallas_call(functools.partial(body, sections, sources), out_shape=(jax...  172 us
    unnamed x7, local copies, waits for them, and re-layouts  5.21 us

profile of v4, /device:TPU:0, one launch (start us, length us, event | category | flops | bytes accessed | tf_op | source)
XLA Modules:
  0.0 178.7 jit_solution(13641310043103296717)
XLA Ops:
  0.6 1.3 convert_bitcast_fusion.gates_ref
  1.9 171.6 %shard_map.76 = (bf16[4,4,1024,512]{3,2,1,0:T(8,128)(2,1)}, bf16[384,4096]{1,0:T(8,128)(2,1)}, bf16[2,576,768]{2,1,0:T(8,128)(2,1)}, f32[8,128]{1,0:T(8,128)}) custom-call(bf16[128,4096]{1,0:T(8,128)(2,1)} %dy_ref.1, s32[8,128]{1,0:T(8,128)} %bitcast.11, f32[8,128]{1,0:T(8,128)} %convert_bitcast_fusion.gates_ref, bf16[2,576,768]{2,1,0:T(8,128)(2,1)} %bitcast.10, ...), custom_call_target="tpu_custom_call" | custom-call | flops 27380416512 | bytes 33554432 | tf_op jit(solution)/shard_map/pallas_call | solution.py:402
  173.5 0.0 copy-start
  173.5 2.9 %copy.11 = bf16[1,2,8,72,768]{4,3,2,1,0:T(8,128)(2,1)} copy(bf16[1,2,8,72,768]{4,3,2,1,0:T(8,128)(2,1)} %bitcast.8) | data formatting | bytes 3538944
  176.5 0.0 copy-done
  176.5 0.0 copy-start.1
  176.5 1.7 copy.12
  178.1 0.0 copy-done.1
  178.2 0.6 copy.13
Async XLA Ops:
  173.5 3.0 %copy-start = (bf16[384,4096]{1,0:T(8,128)(2,1)S(1)}, bf16[384,4096]{1,0:T(8,128)(2,1)}, u32[]{:S(2)}) copy-start(bf16[384,4096]{1,0:T(8,128)(2,1)} %get-tuple-element.7) | copy-start | bytes 9437188
  176.5 1.7 copy-start.1

commit v5 on v4

--- a/solution.py
+++ b/solution.py
@@ -9,6 +9,12 @@
 
 MESH = pl.DeviceIdType.MESH
 TILE = 512
+
+
+def chunk_spans(width):
+    half = width // 2
+    spans = [(at, TILE) for at in range(0, half - TILE, TILE)]
+    return spans + [(half - TILE, TILE // 2), (half - TILE // 2, TILE // 2)]
 
 
 def flipped(index, bits):
@@ -38,7 +44,8 @@
     part_rows = held * part_width
     expert_count = held * sources
     half_rows = tok // 2
-    chunks = tok_ref.shape[0]
+    spans = chunk_spans(width)
+    chunks = len(spans)
     hops = sections - 1
     q = (j % 2) * pairs + j // 2
     bits = [1 << b for b in range(sources.bit_length() - 1)]
@@ -55,12 +62,21 @@
         return pl.ds(pl.multiple_of(place * tok + start, 16), count)
 
     def columns(k):
-        return pl.ds(pl.multiple_of(half * (width // 2) + k * TILE, TILE), TILE)
+        at, size = spans[k]
+        return pl.ds(pl.multiple_of(half * (width // 2) + at, TILE // 2), size)
+
+    def local_columns(k):
+        return pl.ds(*spans[k])
 
     def remote(source, target, send, recv, to):
         return pltpu.make_async_remote_copy(
             source, target, send, recv, device_id=to, device_id_type=MESH)
 
+    barrier = pltpu.get_barrier_semaphore()
+    for d in range(1, sections):
+        pl.semaphore_signal(barrier, inc=1, device_id=((z + d) % sections, j), device_id_type=MESH)
+    for r in range(1, sources):
+        pl.semaphore_signal(barrier, inc=1, device_id=(z, (j + r) % sources), device_id_type=MESH)
     expert_row = lax.broadcasted_iota(jnp.int32, (expert_count, tok), 0)
     named = jnp.zeros((expert_count, tok), f32)
     gate = jnp.zeros((expert_count, tok), f32)
@@ -75,11 +91,6 @@
     tabs[z, q, :expert_count] = jnp.where(named > 0, rank, -1.0)
     tabs[z, q, expert_count:] = gate
 
-    barrier = pltpu.get_barrier_semaphore()
-    for d in range(1, sections):
-        pl.semaphore_signal(barrier, inc=1, device_id=((z + d) % sections, j), device_id_type=MESH)
-    for r in range(1, sources):
-        pl.semaphore_signal(barrier, inc=1, device_id=(z, (j + r) % sources), device_id_type=MESH)
     pl.semaphore_wait(barrier, sections + sources - 2)
 
     own_dy = pltpu.make_async_copy(dy_ref, dy_vm.at[rows_at(q, 0, tok)], local_sem.at[0])
@@ -128,7 +139,7 @@
         s = (z - r + sections if way == 0 else z + r) % sections
         to = ((z + 1 if way == 0 else z - 1 + sections) % sections, j)
         low = q // 2 * 2
-        target = tok_ref.at[k, s, rows_at(low, 0, 2 * tok)]
+        target = tok_ref.at[s, rows_at(low, 0, 2 * tok), local_columns(k)]
         source = dy_vm.at[rows_at(low, 0, 2 * tok), columns(k)] if r == 0 else target
         made = [remote(source, target, z_send.at[k, way, r], z_recv.at[k, way, r], to)]
         if k == 0:
@@ -142,7 +153,7 @@
         bit = bits[b]
         to = device(flipped(q, [bit]))
         low = q // bit * bit
-        target = tok_ref.at[k, s, rows_at(low, 0, bit * tok)]
+        target = tok_ref.at[s, rows_at(low, 0, bit * tok), local_columns(k)]
         made = [remote(target, target, s_send.at[k, way, r, b], s_recv.at[k, way, r, b], to)]
         if k == 0:
             table = tabs.at[s, pl.ds(low, bit)]
@@ -186,12 +197,12 @@
     def gate_row(s, p, expert):
         return row_of(s, p, expert_count + expert)
 
-    def chosen(s, p, expert):
+    def chosen(s, p, expert, before=0, count=pair_rows):
         rank = row_of(s, p, expert)
         lane = lax.broadcasted_iota(jnp.int32, rank.shape, 1)
         rank = jnp.where(rank < 0, -1.0, rank + jnp.where(lane < tok, 0.0, float(capacity)))
-        place = lax.broadcasted_iota(jnp.int32, (pair_rows, 2 * tok), 0).astype(f32)
-        return place == rank
+        place = lax.broadcasted_iota(jnp.int32, (count, 2 * tok), 0).astype(f32)
+        return place == jnp.where(rank < 0, -1.0, rank + float(before))
 
     def scatter_part():
         mate_index = index_of(flipped(q, [1]))
@@ -200,13 +211,15 @@
             s = (z + i) % sections
             for o, first in ((0, j * held), (1, mate_index * held)):
                 for p in range(pairs):
-                    hid = parts[o, s, p * pair_rows:(p + 1) * pair_rows, :]
+                    low = p * pair_rows // 128 * 128
+                    high = -(-(p + 1) * pair_rows // 128) * 128
                     for e in range(held):
-                        gates = jnp.where(
-                            chosen(s, p, first + e), gate_row(s, p, first + e), 0.0).astype(bf16)
+                        here = chosen(s, p, first + e, p * pair_rows - low, high - low)
+                        gates = jnp.where(here, gate_row(s, p, first + e), 0.0).astype(bf16)
+                        at = o * part_rows + e * part_width
                         rows = slice(e * part_width, (e + 1) * part_width)
-                        moved = dot(hid, gates, ((0,), (0,)))[rows].astype(bf16)
-                        at = o * part_rows + e * part_width
+                        moved = dot(
+                            parts[o, s, rows, low:high], gates, ((1,), (0,))).astype(bf16)
                         for c in range(2):
                             start = pl.multiple_of(i * (sources * tok) + (c * pairs + p) * tok, tok)
                             scattered[at:at + part_width, pl.ds(start, tok)] = (
@@ -217,34 +230,55 @@
 
     o_copies = []
 
-    def weight_chunk(k):
-        def fetch(i):
-            return pltpu.make_async_copy(
-                tok_ref.at[k, (z + i) % sections], near.at[i % 2], fetch_sem.at[i % 2])
-
-        if sections > 1:
-            fetch(1).start()
-        acc[...] = dot(scattered[:, :sources * tok], dy_vm[:, columns(k)], ((1,), (0,)))
+    def fetch(k, i):
+        size = spans[k][1]
+        return pltpu.make_async_copy(
+            tok_ref.at[(z + i) % sections, :, local_columns(k)],
+            near.at[i % 2, :, pl.ds(0, size)], fetch_sem.at[i % 2])
+
+    def add_section(k, i):
+        size = spans[k][1]
+        start = i * (sources * tok)
+        if not isinstance(i, int):
+            start = pl.multiple_of(start, tok)
+        acc[:, :size] += dot(
+            scattered[:, pl.ds(start, sources * tok)], near[i % 2, :, :size], ((1,), (0,)))
+
+    def weight_own(k):
+        acc[:, :spans[k][1]] = dot(
+            scattered[:, :sources * tok], dy_vm[:, columns(k)], ((1,), (0,)))
+
+    def weight_late(k, way, r):
+        i = sections - 1 - r if way == 0 else 1 + r
+        fetch(k, i).start()
+        fetch(k, i).wait()
+        add_section(k, i)
+
+    def weight_rest(k):
+        fetch(k, 1).start()
+        weight_own(k)
 
         def one(i, _):
-            fetch(i).wait()
+            fetch(k, i).wait()
 
             @pl.when(i + 1 < sections)
             def _():
-                fetch(i + 1).start()
-
-            start = pl.multiple_of(i * (sources * tok), tok)
-            acc[...] += dot(
-                scattered[:, pl.ds(start, sources * tok)], near[i % 2], ((1,), (0,)))
+                fetch(k, i + 1).start()
+
+            add_section(k, i)
             return 0
 
         lax.fori_loop(1, sections, one, 0)
-        partner_rows[k] = acc[part_rows:].astype(bf16)
+
+    def weight_out(k):
+        size = spans[k][1]
+        partner_rows[:, local_columns(k)] = acc[part_rows:, :size].astype(bf16)
         copy = remote(
-            partner_rows.at[k], dw_ref.at[:, columns(k)], o_send.at[k], o_recv.at[k], mate)
+            partner_rows.at[:, local_columns(k)], dw_ref.at[:, columns(k)],
+            o_send.at[k], o_recv.at[k], mate)
         copy.start()
         o_copies.append(copy)
-        dw_ref[:, columns(k)] = acc[:part_rows].astype(bf16)
+        dw_ref[:, columns(k)] = acc[:part_rows, :size].astype(bf16)
 
     b_copies = []
     for r in range(1, sources):
@@ -313,9 +347,11 @@
     begin(0)
     own_dy.start()
     get_w(0).start()
+    if blocks_ref.shape[2] > slot_rows:
+        blocks_ref[...] = jnp.zeros(blocks_ref.shape, bf16)
     for s in range(sections):
         for e in range(held):
-            blocks_ref[s, :, e * part_width:(e + 1) * part_width] = (
+            blocks_ref[s, e * part_width:(e + 1) * part_width, :slot_rows] = jnp.transpose(
                 hid_ref[e, :, s * part_width:(s + 1) * part_width])
     start_all(h_copies[1:])
     parts[0, z] = blocks_ref[z]
@@ -358,13 +394,24 @@
 
                 each_way(present, r, pass_on)
         some(2)
-        if t >= last and (t - last + 1) % hops == 0:
-            if not built:
-                for copy in x_copies:
-                    copy.wait_recv()
-                scatter_part()
-                built = True
-            weight_chunk((t - last) // hops)
+        if t < last:
+            continue
+        k, r = units[t - last]
+        if not built and r == hops - 1:
+            for copy in x_copies:
+                copy.wait_recv()
+            scatter_part()
+            built = True
+        if k < chunks - 1:
+            if r == hops - 1:
+                weight_rest(k)
+                weight_out(k)
+                if k == chunks - 2:
+                    weight_own(k + 1)
+        else:
+            each_way(present, r, lambda way: weight_late(k, way, r))
+            if r == hops - 1:
+                weight_out(k)
     some(len(work))
     for copy in b_copies:
         copy.wait()
@@ -389,9 +436,9 @@
     tok, width = dy.shape
     held, slot_rows, hidden_width = hid.shape
     part_rows = held * hidden_width // sections
-    blocks = (sections, slot_rows, part_rows)
+    blocks = (sections, part_rows, -(-slot_rows // 128) * 128)
     pairs = sources // 2
-    chunks = width // 2 // TILE
+    chunks = len(chunk_spans(width))
     stages = sources.bit_length() - 1
     any_space, vmem = pl.BlockSpec(memory_space=pl.ANY), pl.BlockSpec(memory_space=pltpu.VMEM)
     dma = pltpu.SemaphoreType.DMA
@@ -402,7 +449,7 @@
     return pl.pallas_call(
         functools.partial(body, sections, sources),
         out_shape=(
-            jax.ShapeDtypeStruct((chunks, sections, sources * tok, TILE), bf16),
+            jax.ShapeDtypeStruct((sections, sources * tok, width // 2), bf16),
             jax.ShapeDtypeStruct((part_rows, width), bf16),
             jax.ShapeDtypeStruct(hid.shape, bf16),
             jax.ShapeDtypeStruct(routes.shape, f32),
@@ -421,7 +468,7 @@
             pltpu.VMEM((held, pairs, slot_rows // pairs, 2 * tok), bf16),
             pltpu.VMEM((slot_rows, TILE), bf16),
             pltpu.VMEM(hid.shape[1:], f32),
-            pltpu.VMEM((chunks, part_rows, TILE), bf16),
+            pltpu.VMEM((part_rows, width // 2), bf16),
             pltpu.VMEM(back, f32),
             pltpu.VMEM(back, f32),
             dma((2,)), dma((2,)), dma((3, sources)), dma((3, sources)),

time: 180 us -> 187 us (1.039)
  Pallas kernels: 172 us -> 179 us
    pallas_call x1, Pallas kernels: 172 us -> 179 us  [fused(): pl.pallas_call(functools.partial(body, sections, sources), out_shape=(jax...]
where the time goes in v5:
time: 187 us; the launch traced here: 186 us
  Pallas kernels  179 us (96%)
  local copies, waits for them, and re-layouts  5.21 us (3%)
    pallas_call x1, Pallas kernels, fused(): pl.pallas_call(functools.partial(body, sections, sources), out_shape=(jax...  179 us
    unnamed x7, local copies, waits for them, and re-layouts  5.21 us

profile of v5, /device:TPU:0, one launch (start us, length us, event | category | flops | bytes accessed | tf_op | source)
XLA Modules:
  0.0 186.1 jit_solution(9325613340488756514)
XLA Ops:
  0.6 1.3 convert_bitcast_fusion.gates_ref
  1.9 178.9 %shard_map.76 = (bf16[4,1024,2048]{2,1,0:T(8,128)(2,1)}, bf16[384,4096]{1,0:T(8,128)(2,1)}, bf16[2,576,768]{2,1,0:T(8,128)(2,1)}, f32[8,128]{1,0:T(8,128)}) custom-call(bf16[128,4096]{1,0:T(8,128)(2,1)} %dy_ref.1, s32[8,128]{1,0:T(8,128)} %bitcast.11, f32[8,128]{1,0:T(8,128)} %convert_bitcast_fusion.gates_ref, bf16[2,576,768]{2,1,0:T(8,128)(2,1)} %bitcast.10, ...), custom_call_target="tpu_custom_call" | custom-call | flops 27380416512 | bytes 33554432 | tf_op jit(solution)/shard_map/pallas_call | solution.py:449
  180.8 0.0 copy-start
  180.8 2.9 %copy.11 = bf16[1,2,8,72,768]{4,3,2,1,0:T(8,128)(2,1)} copy(bf16[1,2,8,72,768]{4,3,2,1,0:T(8,128)(2,1)} %bitcast.8) | data formatting | bytes 3538944
  183.8 0.0 copy-done
  183.8 0.0 copy-start.1
  183.8 1.7 copy.12
  185.5 0.0 copy-done.1
  185.5 0.6 copy.13
Async XLA Ops:
  180.8 3.0 %copy-start = (bf16[384,4096]{1,0:T(8,128)(2,1)S(1)}, bf16[384,4096]{1,0:T(8,128)(2,1)}, u32[]{:S(2)}) copy-start(bf16[384,4096]{1,0:T(8,128)(2,1)} %get-tuple-element.7) | copy-start | bytes 9437188
  183.8 1.7 copy-start.1
